TPU v7x, 32 devices: a whole 2x2x4 slice. The times are simulated.
32 devices in a mesh: dp: 4 (over z), ctx: 8 (over y, x, core).
Axes of the slice: x: 2, y: 2, z: 4, core: 2. Of those that a mesh axis runs over, the one named last changes fastest.
Arguments:
- frames: bfloat16 [4, 1024, 512], P('dp', 'ctx'), may hold values from -6 to 6
- conv_weight: bfloat16 [3, 512, 512], replicated, may hold values from -0.15625 to 0.15625
- proj_weight: bfloat16 [512, 768], replicated, may hold values from -0.25 to 0.25
- query_weight: bfloat16 [768, 384], replicated, may hold values from -1.5 to 1.5
- key_weight: bfloat16 [768, 384], replicated, may hold values from -1.5 to 1.5
- value_weight: bfloat16 [768, 384], replicated, may hold values from -0.21875 to 0.21875
- cotangent: bfloat16 [4, 512, 384], P('dp', 'ctx'), may hold values from -6 to 6
Outputs:
- weight_grad: float32 [1536, 512], P('ctx', 'dp')
- frame_grad: bfloat16 [4, 1024, 512], P('dp', 'ctx')
All inputs are finite; a program needn't handle non-finite values.
Results may differ from a plain program's by a relative error of at most 0.04.
Values may be sent and summed in bfloat16 or wider, within the bound.
A program may use at most 64 MiB of HBM per device.

v0:
```python
import math
import jax
import jax.numpy as jnp
from jax import lax
from jax.sharding import PartitionSpec as P

HEADS = 6
HEAD_DIM = 64
SQRT_HALF = 0.7071067811865476
INV_ROOT_TAU = 0.3989422804014327
EPSILON = 1e-05


def from_behind(value, axis, steps):
    count = lax.axis_size(axis)
    initial, last = (max(0, -steps), min(count, count - steps))
    return lax.ppermute(value, axis, [(source, source + steps) for source in range(initial, last)])


def gelu_slope(pre):
    return 0.5 * (1.0 + lax.erf(pre * SQRT_HALF)) + pre * INV_ROOT_TAU * jnp.exp(-0.5 * pre * pre)


def blocked(step_fn, carry, piece):
    rows = piece[0].shape[0]
    block_rows = math.gcd(rows, 512)
    block_count = rows // block_rows
    stacked = tuple(
        (member.reshape((block_count, block_rows) + member.shape[1:]) for member in piece)
    )

    def inner(state, item):
        block_index, members = item
        return (step_fn(state, members, block_index * block_rows), None)

    final, unused = lax.scan(inner, carry, (jnp.arange(block_count, dtype=jnp.int32), stacked))
    return final


def local(frames, conv_weight, proj_weight, query_weight, key_weight, value_weight, cotangent):
    inputs = frames[0]
    count = inputs.shape[0] // 2
    width = inputs.shape[1]
    following = from_behind(inputs[:1], "ctx", -1)
    paired = inputs.reshape(count, 2, width)
    tap_first = paired[:, 0]
    tap_second = paired[:, 1]
    tap_third = jnp.concatenate([tap_first[1:], following], 0)
    conv_out = jnp.dot(tap_first, conv_weight[0], preferred_element_type=jnp.float32)
    conv_out = conv_out + jnp.dot(tap_second, conv_weight[1], preferred_element_type=jnp.float32)
    conv_out = conv_out + jnp.dot(tap_third, conv_weight[2], preferred_element_type=jnp.float32)
    activated = jax.nn.gelu(conv_out, approximate=False)
    centre = jnp.mean(activated, -1, keepdims=True)
    spread = jnp.mean((activated - centre) ** 2, -1, keepdims=True)
    inv_std = lax.rsqrt(spread + EPSILON)
    normed = (activated - centre) * inv_std
    hidden = jnp.dot(
        normed.astype(jnp.bfloat16), proj_weight, preferred_element_type=jnp.float32
    ).astype(jnp.bfloat16)
    queries = jnp.dot(hidden, query_weight, preferred_element_type=jnp.float32).astype(jnp.bfloat16)
    keys = jnp.dot(hidden, key_weight, preferred_element_type=jnp.float32).astype(jnp.bfloat16)
    values = jnp.dot(hidden, value_weight, preferred_element_type=jnp.float32).astype(jnp.bfloat16)
    upstream = cotangent[0]
    scale = HEAD_DIM ** (-0.5)
    query_heads = queries.reshape(count, HEADS, HEAD_DIM)
    key_heads = keys.reshape(count, HEADS, HEAD_DIM)
    value_heads = values.reshape(count, HEADS, HEAD_DIM)
    grad_heads = upstream.reshape(count, HEADS, HEAD_DIM)

    def forward_block(carry, piece, start):
        running_top, running_total, accum = carry
        rows = piece[0].shape[0]
        keys_part = piece[0].reshape(rows, HEADS, HEAD_DIM)
        values_part = piece[1].reshape(rows, HEADS, HEAD_DIM)
        scores = (
            jnp.einsum("qhe,khe->hqk", query_heads, keys_part, preferred_element_type=jnp.float32)
            * scale
        )
        new_top = jnp.maximum(running_top, jnp.max(scores, -1))
        factor = jnp.exp(running_top - new_top)
        weights = jnp.exp(scores - new_top[:, :, None])
        new_total = running_total * factor + jnp.sum(weights, -1)
        new_accum = accum * jnp.transpose(factor)[:, :, None] + jnp.einsum(
            "hqk,khe->qhe",
            weights,
            values_part.astype(jnp.float32),
            precision=lax.Precision.HIGHEST,
        )
        return (new_top, new_total, new_accum)

    start_state = (
        jnp.full((HEADS, count), -jnp.inf, jnp.float32),
        jnp.zeros((HEADS, count), jnp.float32),
        jnp.zeros((count, HEADS, HEAD_DIM), jnp.float32),
    )
    final_top, final_total, final_accum = blocked(
        forward_block,
        start_state,
        (
            lax.all_gather(keys, "ctx", axis=0, tiled=True),
            lax.all_gather(values, "ctx", axis=0, tiled=True),
        ),
    )
    lse_heads = final_top + jnp.log(final_total)
    outputs = final_accum / jnp.transpose(final_total)[:, :, None]
    delta_rows = jnp.sum(grad_heads.astype(jnp.float32) * outputs, -1)
    delta_heads = jnp.transpose(delta_rows)

    def query_block(carry, piece, start):
        rows = piece[0].shape[0]
        keys_part = piece[0].reshape(rows, HEADS, HEAD_DIM)
        values_part = piece[1].reshape(rows, HEADS, HEAD_DIM)
        scores = (
            jnp.einsum("qhe,khe->hqk", query_heads, keys_part, preferred_element_type=jnp.float32)
            * scale
        )
        probs = jnp.exp(scores - lse_heads[:, :, None])
        prob_grad = jnp.einsum(
            "qhe,khe->hqk", grad_heads, values_part, preferred_element_type=jnp.float32
        )
        score_grad = probs * (prob_grad - delta_heads[:, :, None])
        return carry + jnp.einsum(
            "hqk,khe->qhe",
            score_grad.astype(jnp.bfloat16),
            keys_part,
            preferred_element_type=jnp.float32,
        )

    query_start = jnp.zeros((count, HEADS, HEAD_DIM), jnp.float32)
    query_accum = blocked(
        query_block,
        query_start,
        (
            lax.all_gather(keys, "ctx", axis=0, tiled=True),
            lax.all_gather(values, "ctx", axis=0, tiled=True),
        ),
    )
    query_grad = (query_accum * scale).astype(jnp.bfloat16).reshape(count, HEADS * HEAD_DIM)
    all_lse, all_delta = (
        lax.all_gather(jnp.transpose(lse_heads), "ctx", axis=0, tiled=True),
        lax.all_gather(delta_rows, "ctx", axis=0, tiled=True),
    )

    def key_block(carry, piece, start):
        key_accum, value_accum = carry
        rows = piece[0].shape[0]
        query_part = piece[0].reshape(rows, HEADS, HEAD_DIM)
        grad_part = piece[1].reshape(rows, HEADS, HEAD_DIM)
        lse_part = jnp.transpose(lax.dynamic_slice_in_dim(all_lse, start, rows, 0))
        delta_part = jnp.transpose(lax.dynamic_slice_in_dim(all_delta, start, rows, 0))
        scores = (
            jnp.einsum("qhe,khe->hqk", query_part, key_heads, preferred_element_type=jnp.float32)
            * scale
        )
        probs = jnp.exp(scores - lse_part[:, :, None])
        value_accum = value_accum + jnp.einsum(
            "hqk,qhe->khe",
            probs.astype(jnp.bfloat16),
            grad_part,
            preferred_element_type=jnp.float32,
        )
        prob_grad = jnp.einsum(
            "qhe,khe->hqk", grad_part, value_heads, preferred_element_type=jnp.float32
        )
        score_grad = probs * (prob_grad - delta_part[:, :, None])
        key_accum = key_accum + jnp.einsum(
            "hqk,qhe->khe",
            score_grad.astype(jnp.bfloat16),
            query_part,
            preferred_element_type=jnp.float32,
        )
        return (key_accum, value_accum)

    key_start = (
        jnp.zeros((count, HEADS, HEAD_DIM), jnp.float32),
        jnp.zeros((count, HEADS, HEAD_DIM), jnp.float32),
    )
    key_accum, value_accum = blocked(
        key_block,
        key_start,
        (
            lax.all_gather(queries, "ctx", axis=0, tiled=True),
            lax.all_gather(upstream, "ctx", axis=0, tiled=True),
        ),
    )
    key_grad = (key_accum * scale).astype(jnp.bfloat16).reshape(count, HEADS * HEAD_DIM)
    value_grad = value_accum.astype(jnp.bfloat16).reshape(count, HEADS * HEAD_DIM)
    hidden_grad = jnp.einsum(
        "tk,dk->td", query_grad, query_weight, preferred_element_type=jnp.float32
    )
    hidden_grad = hidden_grad + jnp.einsum(
        "tk,dk->td", key_grad, key_weight, preferred_element_type=jnp.float32
    )
    hidden_grad = hidden_grad + jnp.einsum(
        "tk,dk->td", value_grad, value_weight, preferred_element_type=jnp.float32
    )
    hidden_grad = hidden_grad.astype(jnp.bfloat16)
    normed_grad = jnp.einsum(
        "td,cd->tc", hidden_grad, proj_weight, preferred_element_type=jnp.float32
    )
    act_grad = inv_std * (
        normed_grad
        - jnp.mean(normed_grad, -1, keepdims=True)
        - normed * jnp.mean(normed_grad * normed, -1, keepdims=True)
    )
    conv_grad = (act_grad * gelu_slope(conv_out)).astype(jnp.bfloat16)
    kernel_terms = jnp.concatenate(
        [
            jnp.einsum("tc,to->co", tap_first, conv_grad, preferred_element_type=jnp.float32),
            jnp.einsum("tc,to->co", tap_second, conv_grad, preferred_element_type=jnp.float32),
            jnp.einsum("tc,to->co", tap_third, conv_grad, preferred_element_type=jnp.float32),
        ],
        0,
    )
    earlier = from_behind(conv_grad[count - 1 :], "ctx", 1)
    first = jnp.einsum("to,co->tc", conv_grad, conv_weight[0], preferred_element_type=jnp.float32)
    second = jnp.einsum("to,co->tc", conv_grad, conv_weight[1], preferred_element_type=jnp.float32)
    third = jnp.einsum("to,co->tc", conv_grad, conv_weight[2], preferred_element_type=jnp.float32)
    incoming = jnp.einsum("to,co->tc", earlier, conv_weight[2], preferred_element_type=jnp.float32)
    moved = jnp.concatenate([incoming, third[:-1]], 0)
    even_rows = first + moved
    frame_rows = jnp.stack([even_rows, second], 1).reshape(2 * count, width).astype(jnp.bfloat16)
    frame_sum = lax.psum_scatter(
        kernel_terms.astype(jnp.bfloat16), "ctx", scatter_dimension=0, tiled=True
    )
    weight_grad = lax.psum_scatter(frame_sum, "dp", scatter_dimension=1, tiled=True).astype(
        jnp.float32
    )
    return (weight_grad, frame_rows[None])


def solution(mesh):
    in_specs = (P("dp", "ctx", None), P(), P(), P(), P(), P(), P("dp", "ctx", None))
    out_specs = (P("ctx", "dp"), P("dp", "ctx", None))
    return jax.shard_map(local, mesh=mesh, in_specs=in_specs, out_specs=out_specs, check_vma=False)
```

profile of v0, /device:TPU:0, one launch (start us, length us, event | category | flops | bytes accessed | tf_op | source)
XLA Modules:
  0.0 179.6 jit_solution(5564387920158402411)
XLA Ops:
  8.0 1.3 collective-permute-start
  9.3 1.0 reshape_squeeze.6
  10.5 1.4 fusion.36
  11.9 1.2 convolution_add_fusion.3
  13.1 12.5 %all-gather = bf16[1,512,384]{2,1,0:T(8,128)(2,1)S(1)} all-gather(bf16[1,64,384]{2,1,0:T(8,128)(2,1)S(1)} %copy-done.17), channel_id=2, replica_groups=mesh['dp'=4,'ctx'=8] {'ctx'}, dimensions={1}, use_global_device_ids=true | all-gather | bytes 442368 | tf_op jit(solution)/shard_map/all_gather | solution.py:183
  27.2 1.2 fusion.90
  30.7 9.7 %all_gather.20 = bf16[512,384]{1,0:T(8,128)(2,1)} all-gather(bf16[64,384]{1,0:T(8,128)(2,1)S(1)} %convolution_convert_fusion.8), channel_id=1, replica_groups=mesh['dp'=4,'ctx'=8] {'ctx'}, dimensions={0}, use_global_device_ids=true | all-gather | bytes 442368 | tf_op jit(solution)/shard_map/all_gather | solution.py:134
  40.3 1.9 %copy.38 = bf16[512,384]{0,1:T(8,128)(2,1)} copy(bf16[512,384]{1,0:T(8,128)(2,1)} %all_gather.20) | data formatting | bytes 786432 | tf_op jit(solution)/shard_map/all_gather | solution.py:134
  43.3 1.4 fusion.93
  45.5 10.4 %all_gather.22 = bf16[512,384]{1,0:T(8,128)(2,1)} all-gather(bf16[64,384]{1,0:T(8,128)(2,1)S(1)} %copy-done.13), channel_id=1, replica_groups=mesh['dp'=4,'ctx'=8] {'ctx'}, dimensions={0}, use_global_device_ids=true | all-gather | bytes 442368 | tf_op jit(solution)/shard_map/all_gather | solution.py:182
  56.0 1.6 reshape.119
  57.6 1.3 convolution_convert_fusion.6
  59.5 9.7 %all_gather.21 = bf16[512,384]{1,0:T(8,128)(2,1)} all-gather(bf16[64,384]{1,0:T(8,128)(2,1)S(1)} %convolution_convert_fusion.6), channel_id=1, replica_groups=mesh['dp'=4,'ctx'=8] {'ctx'}, dimensions={0}, use_global_device_ids=true | all-gather | bytes 442368 | tf_op jit(solution)/shard_map/all_gather | solution.py:135
  69.2 1.6 reshape.120
  70.8 1.9 %copy.40 = bf16[512,384]{0,1:T(8,128)(2,1)} copy(bf16[512,384]{1,0:T(8,128)(2,1)} %all_gather.21) | data formatting | bytes 786432 | tf_op jit(solution)/shard_map/all_gather | solution.py:135
  72.7 1.7 fusion.20
  74.4 2.3 %fusion.19 = bf16[6,64,64]{2,1,0:T(8,128)(2,1)} fusion(bf16[512,6,64]{0,2,1:T(8,128)(2,1)} %bitcast.157, bf16[512,6,64]{0,2,1:T(8,128)(2,1)} %bitcast.161, bf16[64,6,64]{0,2,1:T(8,128)(2,1)} %bitcast.166, f32[6,64,512]{2,1,0:T(8,128)S(1)} %get-tuple-element.67, f32[6,64]{1,0:T(8,128)S(1)} %bitcast.170, f32[6,64]{1,0:T(8,128)S(1)} %log_add_fusion), kind=kOutput, calls=%fused_computation.30 | convolution fusion | flops 51167232 | bytes 1674240 | tf_op jit(solution)/shard_map/while/body/eval_jaxpr/hqk,khe->qhe/dot_general | solution.py:122
  76.7 2.1 %fusion.96 = f32[64,768]{1,0:T(8,128)} fusion(bf16[64,384]{0,1:T(8,128)(2,1)} %bitcast.164, bf16[768,384]{1,0:T(8,128)(2,1)} %param.10), kind=kOutput, calls=%fused_computation.137 | convolution fusion | flops 37748736 | bytes 835584 | tf_op jit(solution)/shard_map/tk,dk->td/dot_general | solution.py:188
  78.8 1.9 %copy.43 = bf16[512,384]{0,1:T(8,128)(2,1)} copy(bf16[512,384]{1,0:T(8,128)(2,1)} %all_gather.22) | data formatting | bytes 786432 | tf_op jit(solution)/shard_map/all_gather | solution.py:182
  80.7 8.9 %all-gather.1 = f32[8,64,6]{1,2,0:T(8,128)S(1)} all-gather(f32[1,64,6]{1,2,0:T(8,128)S(1)} %get-tuple-element.62), channel_id=1, replica_groups=mesh['dp'=4,'ctx'=8] {'ctx'}, dimensions={0}, use_global_device_ids=true | all-gather | bytes 13824 | tf_op jit(solution)/shard_map/all_gather | solution.py:140
  90.4 8.2 %all-gather.2 = f32[8,64,6]{1,2,0:T(8,128)S(1)} all-gather(f32[1,64,6]{1,2,0:T(8,128)S(1)} %bitcast.171), channel_id=1, replica_groups=mesh['dp'=4,'ctx'=8] {'ctx'}, dimensions={0}, use_global_device_ids=true | all-gather | bytes 13824 | tf_op jit(solution)/shard_map/all_gather | solution.py:141
  98.6 1.3 fusion.1
  100.9 1.7 reshape.123
  102.6 2.1 %fusion.18 = bf16[6,64,64]{2,1,0:T(8,128)(2,1)} fusion(bf16[512,6,64]{0,2,1:T(8,128)(2,1)} %bitcast.155, f32[6,512,64]{1,2,0:T(8,128)S(1)} %fusion.1, bf16[512,6,64]{0,2,1:T(8,128)(2,1)S(1)} %bitcast.153, f32[6,512]{1,0:T(8,128)S(1)} %bitcast.167, bf16[64,6,64]{2,1,0:T(8,128)(2,1)} %reshape.120), kind=kOutput, calls=%fused_computation.29 | convolution fusion | flops 50970624 | bytes 1683456 | tf_op jit(solution)/shard_map/while/body/eval_jaxpr/hqk,qhe->khe/dot_general | solution.py:166
  104.6 1.5 convolution_add_fusion.1
  106.2 1.8 fusion.89
  109.2 1.3 pad_maximum_fusion
  110.5 2.2 %collective-permute-start.1 = (bf16[1,512]{1,0:T(2,128)(2,1)S(1)}, bf16[1,512]{1,0:T(2,128)(2,1)S(1)}, u32[]{:S(2)}, u32[]{:S(2)}) collective-permute-start(bf16[1,512]{1,0:T(2,128)(2,1)S(1)} %slice.53), channel_id=1, source_target_pairs={{0,1},{1,2},{2,3},{3,4},{4,5},{5,6},{6,7},{8,9},{9,10},{10,11},{11... | collective-permute-start | bytes 3080 | tf_op jit(solution)/shard_map/ppermute | solution.py:17
  113.3 36.0 %reduce-scatter.5.cloned.1.call-done = bf16[192,512]{1,0:T(8,128)(2,1)} async-done(((bf16[1536,512]{1,0:T(8,128)(2,1)}), bf16[192,512]{1,0:T(8,128)(2,1)}) %reduce-scatter.5.cloned.1.call-update) | async-done | bytes 196624 | tf_op jit(solution)/shard_map/reduce_scatter | solution.py:223
  149.4 1.8 copy.52
  152.6 18.6 %reduce-scatter.7.cloned.1.call-done = bf16[128,192]{1,0:T(8,128)(2,1)} async-done(((bf16[512,192]{1,0:T(8,128)(2,1)}), bf16[128,192]{1,0:T(8,128)(2,1)}) %reduce-scatter.7.cloned.1.call-update) | async-done | bytes 49168
  171.2 0.9 copy.53
  (92 shorter events, 12.8 us)
Async XLA Ops:
  7.2 22.3 %copy-start = (bf16[512,768]{1,0:T(8,128)(2,1)S(1)}, bf16[512,768]{1,0:T(8,128)(2,1)}, u32[]{:S(2)}) copy-start(bf16[512,768]{1,0:T(8,128)(2,1)} %param.9) | copy-start | bytes 2359300
  7.2 5.9 %copy-start.17 = (bf16[1,64,384]{2,1,0:T(8,128)(2,1)S(1)}, bf16[1,64,384]{2,1,0:T(8,128)(2,1)}, u32[]{:S(2)}) copy-start(bf16[1,64,384]{2,1,0:T(8,128)(2,1)} %param.13) | copy-start | bytes 147460
  7.2 142.2 %reduce-scatter.5.cloned.1.call-start = ((), (), s32[]{:S(2)}) async-start(), calls=%async_computation.2 | async-start | bytes 1769472 | tf_op jit(solution)/shard_map/reduce_scatter | solution.py:223
  8.0 18.7 %collective-permute-start = (bf16[1,512]{1,0:T(2,128)(2,1)S(1)}, bf16[1,512]{1,0:T(2,128)(2,1)S(1)}, u32[]{:S(2)}, u32[]{:S(2)}) collective-permute-start(bf16[1,512]{1,0:T(2,128)(2,1)S(1)} %slice_bitcast_fusion), channel_id=1, source_target_pairs={{1,0},{2,1},{3,2},{4,3},{5,4},{6,5},{7,6},{9,8},{10,9},{11,10},{12... | collective-permute-start | bytes 3080 | tf_op jit(solution)/shard_map/ppermute | solution.py:17
  10.4 1.4 copy-start.7
  10.5 2.7 %copy-start.9 = (bf16[64,1,512]{2,1,0:T(2,128)(2,1)}, bf16[64,1,512]{2,1,0:T(2,128)(2,1)S(1)}, u32[]{:S(2)}) copy-start(bf16[64,1,512]{2,1,0:T(2,128)(2,1)S(1)} %get-tuple-element.60) | copy-start | bytes 196612
  10.5 16.7 %copy-start.1 = (bf16[3,512,512]{2,1,0:T(8,128)(2,1)S(1)}, bf16[3,512,512]{2,1,0:T(8,128)(2,1)}, u32[]{:S(2)}) copy-start(bf16[3,512,512]{2,1,0:T(8,128)(2,1)} %param.8) | copy-start | bytes 4718596
  26.5 0.6 copy-start.15
  26.7 1.6 copy-start.23
  27.2 2.6 %copy-start.3 = (bf16[768,384]{1,0:T(8,128)(2,1)S(1)}, bf16[768,384]{1,0:T(8,128)(2,1)}, u32[]{:S(2)}) copy-start(bf16[768,384]{1,0:T(8,128)(2,1)} %param.11) | copy-start | bytes 1769476
  28.4 1.7 copy-start.4
  28.4 13.9 %copy-start.2 = (bf16[768,384]{1,0:T(8,128)(2,1)S(1)}, bf16[768,384]{1,0:T(8,128)(2,1)}, u32[]{:S(2)}) copy-start(bf16[768,384]{1,0:T(8,128)(2,1)} %param.10) | copy-start | bytes 1769476
  28.4 0.6 copy-start.19
  29.0 0.5 copy-start.21
  29.8 13.5 %copy-start.6 = (bf16[64,768]{1,0:T(8,128)(2,1)}, bf16[64,768]{1,0:T(8,128)(2,1)S(1)}, u32[]{:S(2)}) copy-start(bf16[64,768]{1,0:T(8,128)(2,1)S(1)} %convolution_convert_fusion.4) | copy-start | bytes 294916
  30.0 0.6 copy-start.11
  42.5 0.8 copy-start.12
  43.3 2.3 %copy-start.13 = (bf16[64,384]{1,0:T(8,128)(2,1)S(1)}, bf16[64,384]{1,0:T(8,128)(2,1)}, u32[]{:S(2)}) copy-start(bf16[64,384]{1,0:T(8,128)(2,1)} %copy-done.12) | copy-start | bytes 147460
  58.9 0.6 copy-start.14
  104.6 3.3 %copy-start.5 = (f32[64,512]{1,0:T(8,128)S(1)}, f32[64,512]{1,0:T(8,128)}, u32[]{:S(2)}) copy-start(f32[64,512]{1,0:T(8,128)} %copy-done.4) | copy-start | bytes 393220
  104.6 3.3 %copy-start.18 = (f32[64,512]{1,0:T(8,128)S(1)}, f32[64,512]{1,0:T(8,128)}, u32[]{:S(2)}) copy-start(f32[64,512]{1,0:T(8,128)} %get-tuple-element.65) | copy-start | bytes 393220
  104.6 3.4 %copy-start.20 = (f32[64]{0:T(128)S(1)}, f32[64]{0:T(128)}, u32[]{:S(2)}) copy-start(f32[64]{0:T(128)} %copy-done.19) | copy-start | bytes 772
  104.6 3.4 %copy-start.22 = (f32[64]{0:T(128)S(1)}, f32[64]{0:T(128)}, u32[]{:S(2)}) copy-start(f32[64]{0:T(128)} %copy-done.21) | copy-start | bytes 772
  104.6 3.5 %copy-start.10 = (bf16[64,1,512]{2,1,0:T(2,128)(2,1)S(1)}, bf16[64,1,512]{2,1,0:T(2,128)(2,1)}, u32[]{:S(2)}) copy-start(bf16[64,1,512]{2,1,0:T(2,128)(2,1)} %copy-done.9) | copy-start | bytes 196612
  106.1 2.3 %copy-start.8 = (bf16[64,1,512]{2,1,0:T(2,128)(2,1)S(1)}, bf16[64,1,512]{2,1,0:T(2,128)(2,1)}, u32[]{:S(2)}) copy-start(bf16[64,1,512]{2,1,0:T(2,128)(2,1)} %copy-done.7) | copy-start | bytes 196612
  106.1 2.7 %copy-start.16 = (bf16[63,1,512]{2,0,1:T(8,128)(2,1)S(1)}, bf16[63,1,512]{2,0,1:T(8,128)(2,1)}, u32[]{:S(2)}) copy-start(bf16[63,1,512]{2,0,1:T(8,128)(2,1)} %copy-done.15) | copy-start | bytes 193540
  106.2 2.7 %copy-start.24 = (bf16[1,512]{1,0:T(2,128)(2,1)S(1)}, bf16[1,512]{1,0:T(2,128)(2,1)}, u32[]{:S(2)}) copy-start(bf16[1,512]{1,0:T(2,128)(2,1)} %copy-done.23) | copy-start | bytes 3076
  110.5 60.7 %reduce-scatter.7.cloned.1.call-start = ((), (), s32[]{:S(2)}) async-start(), calls=%async_computation.3 | async-start | bytes 327680
  110.5 40.6 %collective-permute-start.1 = (bf16[1,512]{1,0:T(2,128)(2,1)S(1)}, bf16[1,512]{1,0:T(2,128)(2,1)S(1)}, u32[]{:S(2)}, u32[]{:S(2)}) collective-permute-start(bf16[1,512]{1,0:T(2,128)(2,1)S(1)} %slice.53), channel_id=1, source_target_pairs={{0,1},{1,2},{2,3},{3,4},{4,5},{5,6},{6,7},{8,9},{9,10},{10,11},{11... | collective-permute-start | bytes 3080 | tf_op jit(solution)/shard_map/ppermute | solution.py:17
Sparse Core Ops, SparseCore 0:
  110.6 38.7 reduce-scatter.4
  151.6 19.5 reduce-scatter.6
where the time goes:
time: 180 us
  blocking collectives  59.4 us (33%)
  waiting for transfers between devices  54.7 us (30%)
  matrix products  22.3 us (12%)
  local copies, waits for them, and re-layouts  21.9 us (12%)
  between operations  14.5 us (8%)
  starting transfers between devices  3.59 us (2%)
  other arithmetic  3.13 us (2%)
    reduce_scatter x1, waiting for transfers between devices, local(): lax.psum_scatter(kernel_terms.astype(jnp.bfloat16), 'ctx', scatter_dimens...  36 us
    unnamed x3, waiting for transfers between devices  18.6 us
    all_gather x1, blocking collectives, local(): lax.all_gather(upstream, 'ctx', axis=0, tiled=True)  12.5 us
    all_gather x1, blocking collectives, local(): lax.all_gather(queries, 'ctx', axis=0, tiled=True)  10.4 us
    all_gather x1, blocking collectives, local(): lax.all_gather(keys, 'ctx', axis=0, tiled=True)  9.66 us
    all_gather x1, blocking collectives, local(): lax.all_gather(values, 'ctx', axis=0, tiled=True)  9.66 us
    all_gather x1, blocking collectives, local(): lax.all_gather(jnp.transpose(lse_heads), 'ctx', axis=0, tiled=True)  8.94 us
    all_gather x1, blocking collectives, local(): lax.all_gather(delta_rows, 'ctx', axis=0, tiled=True)  8.18 us
  transfers between devices with their start and end apart: 4, of which 2 were waited for; matrix products, arithmetic and copies ran while one was open for 5% of the time, Pallas kernels for 0%

commit v1 on v0

--- a/solution.py
+++ b/solution.py
@@ -9,6 +9,22 @@
 SQRT_HALF = 0.7071067811865476
 INV_ROOT_TAU = 0.3989422804014327
 EPSILON = 1e-05
+
+
+def collect(x, axis, dim):
+    ways, here, step = (lax.axis_size(axis), lax.axis_index(axis), x.shape[dim])
+    shape = [n * ways if d == dim else n for d, n in enumerate(x.shape)]
+    full = lax.dynamic_update_slice_in_dim(jnp.zeros(shape, x.dtype), x, here * step, axis=dim)
+    going_up = going_down = x
+    for far in range(1, ways // 2 + 1):
+        going_up = lax.ppermute(going_up, axis, [(d, (d + 1) % ways) for d in range(ways)])
+        full = lax.dynamic_update_slice_in_dim(full, going_up, (here - far) % ways * step, axis=dim)
+        if 2 * far < ways:
+            going_down = lax.ppermute(going_down, axis, [(d, (d - 1) % ways) for d in range(ways)])
+            full = lax.dynamic_update_slice_in_dim(
+                full, going_down, (here + far) % ways * step, axis=dim
+            )
+    return full
 
 
 def from_behind(value, axis, steps):
@@ -137,7 +153,7 @@
     )
     query_grad = (query_accum * scale).astype(jnp.bfloat16).reshape(count, HEADS * HEAD_DIM)
     all_lse, all_delta = (
-        lax.all_gather(jnp.transpose(lse_heads), "ctx", axis=0, tiled=True),
+        collect(jnp.transpose(lse_heads), "ctx", 0),
         lax.all_gather(delta_rows, "ctx", axis=0, tiled=True),
     )
 

time: 180 us -> 187 us (1.039)
  local copies, waits for them, and re-layouts: 21.9 us -> 30.4 us
  starting transfers between devices: 3.59 us -> 11.7 us
  blocking collectives: 59.4 us -> 51.7 us
  matrix products: 22.3 us -> 19.2 us
    all_gather x1 -> x0, blocking collectives: 8.94 us -> none  [local(): lax.all_gather(jnp.transpose(lse_heads), 'ctx', axis=0, tiled=True)]
    ppermute x0 -> x7, starting transfers between devices: none -> 8.04 us  [the longest x3 7.28 us: collect(): lax.ppermute(going_down, axis, [(d, (d - 1) % ways) for d in range(ways)])]
    dynamic_update_slice x0 -> x8, local copies, waits for them, and re-layouts: none -> 6.64 us  [the longest x4 3.32 us: collect(): lax.dynamic_update_slice_in_dim(full, going_up, (here - far) % ways * ste...]
    all_gather x1, blocking collectives: 8.18 us -> 10.2 us  [local(): lax.all_gather(delta_rows, 'ctx', axis=0, tiled=True)]
    unnamed x56 -> x59, local copies, waits for them, and re-layouts: 6.82 us -> 8.17 us
  transfers between devices with their start and end apart: 4 -> 11, of which waited for: 2 -> 3; matrix products, arithmetic and copies ran while one was open for 5% -> 16% of each run, Pallas kernels for 0% -> 0%
where the time goes in v1:
time: 187 us; the launch traced here: 185 us
  waiting for transfers between devices  54.6 us (29%)
  blocking collectives  51.7 us (28%)
  local copies, waits for them, and re-layouts  30.4 us (16%)
  matrix products  19.2 us (10%)
  between operations  14.6 us (8%)
  starting transfers between devices  11.7 us (6%)
  other arithmetic  3.13 us (2%)
    reduce_scatter x1, waiting for transfers between devices, local(): lax.psum_scatter(kernel_terms.astype(jnp.bfloat16), 'ctx', scatter_dimens...  35.8 us
    unnamed x3, waiting for transfers between devices  18.7 us
    all_gather x1, blocking collectives, local(): lax.all_gather(upstream, 'ctx', axis=0, tiled=True)  12.5 us
    all_gather x1, blocking collectives, local(): lax.all_gather(values, 'ctx', axis=0, tiled=True)  10.3 us
    all_gather x1, blocking collectives, local(): lax.all_gather(delta_rows, 'ctx', axis=0, tiled=True)  10.2 us
    all_gather x1, blocking collectives, local(): lax.all_gather(keys, 'ctx', axis=0, tiled=True)  9.82 us
    all_gather x1, blocking collectives, local(): lax.all_gather(queries, 'ctx', axis=0, tiled=True)  8.84 us
    unnamed x59, local copies, waits for them, and re-layouts  8.17 us
  transfers between devices with their start and end apart: 11, of which 3 were waited for; matrix products, arithmetic and copies ran while one was open for 16% of the time, Pallas kernels for 0%

profile of v1, /device:TPU:0, one launch (start us, length us, event | category | flops | bytes accessed | tf_op | source)
XLA Modules:
  0.0 185.3 jit_solution(2318902725415570372)
XLA Ops:
  8.1 1.3 collective-permute-start
  9.4 1.0 reshape_squeeze.6
  10.7 1.5 copy.41
  12.2 12.5 %all-gather = bf16[1,512,384]{2,1,0:T(8,128)(2,1)S(1)} all-gather(bf16[1,64,384]{2,1,0:T(8,128)(2,1)} %param.13), channel_id=2, replica_groups=mesh['dp'=4,'ctx'=8] {'ctx'}, dimensions={1}, use_global_device_ids=true | all-gather | bytes 442368 | tf_op jit(solution)/shard_map/all_gather | solution.py:199
  25.8 1.2 fusion.90
  29.3 9.8 %all_gather.17 = bf16[512,384]{1,0:T(8,128)(2,1)} all-gather(bf16[64,384]{1,0:T(8,128)(2,1)S(1)} %convolution_convert_fusion.8), channel_id=1, replica_groups=mesh['dp'=4,'ctx'=8] {'ctx'}, dimensions={0}, use_global_device_ids=true | all-gather | bytes 442368 | tf_op jit(solution)/shard_map/all_gather | solution.py:150
  39.1 1.9 %copy.38 = bf16[512,384]{0,1:T(8,128)(2,1)} copy(bf16[512,384]{1,0:T(8,128)(2,1)} %all_gather.17) | data formatting | bytes 786432 | tf_op jit(solution)/shard_map/all_gather | solution.py:150
  42.0 1.4 fusion.93
  44.8 2.3 %collective-permute-start.2 = (f32[64,6]{0,1:T(8,128)S(1)}, f32[64,6]{0,1:T(8,128)}, u32[]{:S(2)}, u32[]{:S(2)}) collective-permute-start(f32[64,6]{0,1:T(8,128)S(1)} %get-tuple-element.62), channel_id=1, source_target_pairs={{0,7},{1,0},{2,1},{3,2},{4,3},{5,4},{6,5},{7,6},{8,15},{9,8},{10,9... | collective-permute-start | bytes 4616 | tf_op jit(solution)/shard_map/ppermute | solution.py:23
  47.9 10.3 %all_gather.18 = bf16[512,384]{1,0:T(8,128)(2,1)} all-gather(bf16[64,384]{1,0:T(8,128)(2,1)S(1)} %convolution_convert_fusion.6), channel_id=1, replica_groups=mesh['dp'=4,'ctx'=8] {'ctx'}, dimensions={0}, use_global_device_ids=true | all-gather | bytes 442368 | tf_op jit(solution)/shard_map/all_gather | solution.py:151
  58.2 1.9 %copy.40 = bf16[512,384]{0,1:T(8,128)(2,1)} copy(bf16[512,384]{1,0:T(8,128)(2,1)} %all_gather.18) | data formatting | bytes 786432 | tf_op jit(solution)/shard_map/all_gather | solution.py:151
  60.1 1.7 fusion.18
  61.8 2.3 %fusion.17 = bf16[6,64,64]{2,1,0:T(8,128)(2,1)} fusion(bf16[512,6,64]{0,2,1:T(8,128)(2,1)} %bitcast.151, bf16[512,6,64]{0,2,1:T(8,128)(2,1)} %bitcast.155, bf16[64,6,64]{0,2,1:T(8,128)(2,1)} %bitcast.162, f32[6,64,512]{2,1,0:T(8,128)S(1)} %get-tuple-element.67, f32[6,64]{1,0:T(8,128)S(1)} %bitcast.165, f32[6,64]{1,0:T(8,128)S(1)} %log_add_fusion), kind=kOutput, calls=%fused_computation.28 | convolution fusion | flops 51167232 | bytes 1674240 | tf_op jit(solution)/shard_map/while/body/eval_jaxpr/hqk,khe->qhe/dot_general | solution.py:138
  64.2 8.8 %all_gather.19 = bf16[512,384]{1,0:T(8,128)(2,1)S(1)} all-gather(bf16[64,384]{1,0:T(8,128)(2,1)} %copy-done.15), channel_id=1, replica_groups=mesh['dp'=4,'ctx'=8] {'ctx'}, dimensions={0}, use_global_device_ids=true | all-gather | bytes 442368 | tf_op jit(solution)/shard_map/all_gather | solution.py:198
  73.0 1.6 reshape.119
  75.9 1.3 convolution_multiply_fusion
  77.2 2.3 %collective-permute-start.4 = (f32[64,6]{0,1:T(8,128)}, f32[64,6]{0,1:T(8,128)}, u32[]{:S(2)}, u32[]{:S(2)}) collective-permute-start(f32[64,6]{0,1:T(8,128)} %collective-permute-done.2), channel_id=1, source_target_pairs={{0,7},{1,0},{2,1},{3,2},{4,3},{5,4},{6,5},{7,6},{8,15},{9,8},{10,9... | collective-permute-start | bytes 4616 | tf_op jit(solution)/shard_map/ppermute | solution.py:23
  79.7 2.1 %fusion.96 = f32[64,768]{1,0:T(8,128)} fusion(bf16[64,384]{0,1:T(8,128)(2,1)} %bitcast.160, bf16[768,384]{1,0:T(8,128)(2,1)} %param.10), kind=kOutput, calls=%fused_computation.137 | convolution fusion | flops 37748736 | bytes 835584 | tf_op jit(solution)/shard_map/tk,dk->td/dot_general | solution.py:204
  81.8 2.6 %collective-permute-start.6 = (f32[64,6]{0,1:T(8,128)}, f32[64,6]{0,1:T(8,128)}, u32[]{:S(2)}, u32[]{:S(2)}) collective-permute-start(f32[64,6]{0,1:T(8,128)} %collective-permute-done.4), channel_id=1, source_target_pairs={{0,7},{1,0},{2,1},{3,2},{4,3},{5,4},{6,5},{7,6},{8,15},{9,8},{10,9... | collective-permute-start | bytes 4616 | tf_op jit(solution)/shard_map/ppermute | solution.py:23
  84.4 10.2 %all-gather.1 = f32[8,64,6]{1,2,0:T(8,128)} all-gather(f32[1,64,6]{1,2,0:T(8,128)S(1)} %bitcast.166), channel_id=1, replica_groups=mesh['dp'=4,'ctx'=8] {'ctx'}, dimensions={0}, use_global_device_ids=true | all-gather | bytes 13824 | tf_op jit(solution)/shard_map/all_gather | solution.py:157
  94.7 1.6 reshape.120
  96.3 1.4 copy.47
  97.6 1.4 reshape.128
  106.7 1.7 reshape.123
  108.3 2.1 %fusion.16 = bf16[6,64,64]{2,1,0:T(8,128)(2,1)} fusion(bf16[512,6,64]{0,2,1:T(8,128)(2,1)} %bitcast.149, bf16[512,6,64]{0,2,1:T(8,128)(2,1)S(1)} %bitcast.147, f32[6,512,64]{1,2,0:T(8,128)S(1)} %convolution_multiply_fusion, f32[6,512]{1,0:T(8,128)} %bitcast.163, f32[6,512]{1,0:T(8,128)S(1)} %bitcast.159, bf16[64,6,64]{2,1,0:T(8,128)(2,1)} %reshape.120), kind=kOutput, calls=%fused_computation.27 | convolution fusion | flops 51167232 | bytes 1695744 | tf_op jit(solution)/shard_map/while/body/eval_jaxpr/hqk,qhe->khe/dot_general | solution.py:182
  110.5 1.5 convolution_add_fusion.1
  112.0 1.8 fusion.89
  115.0 1.3 pad_maximum_fusion
  116.4 2.3 %collective-permute-start.8 = (bf16[1,512]{1,0:T(2,128)(2,1)S(1)}, bf16[1,512]{1,0:T(2,128)(2,1)S(1)}, u32[]{:S(2)}, u32[]{:S(2)}) collective-permute-start(bf16[1,512]{1,0:T(2,128)(2,1)S(1)} %slice.53), channel_id=1, source_target_pairs={{0,1},{1,2},{2,3},{3,4},{4,5},{5,6},{6,7},{8,9},{9,10},{10,11},{11... | collective-permute-start | bytes 3080 | tf_op jit(solution)/shard_map/ppermute | solution.py:33
  119.2 35.8 %reduce-scatter.5.cloned.1.call-done = bf16[192,512]{1,0:T(8,128)(2,1)} async-done(((bf16[1536,512]{1,0:T(8,128)(2,1)}), bf16[192,512]{1,0:T(8,128)(2,1)}) %reduce-scatter.5.cloned.1.call-update) | async-done | bytes 196624 | tf_op jit(solution)/shard_map/reduce_scatter | solution.py:239
  155.0 1.8 copy.51
  158.2 18.7 %reduce-scatter.7.cloned.1.call-done = bf16[128,192]{1,0:T(8,128)(2,1)} async-done(((bf16[512,192]{1,0:T(8,128)(2,1)}), bf16[128,192]{1,0:T(8,128)(2,1)}) %reduce-scatter.7.cloned.1.call-update) | async-done | bytes 49168
  (116 shorter events, 21.3 us)
Async XLA Ops:
  7.2 20.9 %copy-start = (bf16[512,768]{1,0:T(8,128)(2,1)S(1)}, bf16[512,768]{1,0:T(8,128)(2,1)}, u32[]{:S(2)}) copy-start(bf16[512,768]{1,0:T(8,128)(2,1)} %param.9) | copy-start | bytes 2359300
  7.2 17.5 %copy-start.1 = (bf16[3,512,512]{2,1,0:T(8,128)(2,1)S(1)}, bf16[3,512,512]{2,1,0:T(8,128)(2,1)}, u32[]{:S(2)}) copy-start(bf16[3,512,512]{2,1,0:T(8,128)(2,1)} %param.8) | copy-start | bytes 4718596
  7.2 147.8 %reduce-scatter.5.cloned.1.call-start = ((), (), s32[]{:S(2)}) async-start(), calls=%async_computation.2 | async-start | bytes 1769472 | tf_op jit(solution)/shard_map/reduce_scatter | solution.py:239
  8.1 17.4 %collective-permute-start = (bf16[1,512]{1,0:T(2,128)(2,1)S(1)}, bf16[1,512]{1,0:T(2,128)(2,1)S(1)}, u32[]{:S(2)}, u32[]{:S(2)}) collective-permute-start(bf16[1,512]{1,0:T(2,128)(2,1)S(1)} %slice_bitcast_fusion), channel_id=1, source_target_pairs={{1,0},{2,1},{3,2},{4,3},{5,4},{6,5},{7,6},{9,8},{10,9},{11,10},{12... | collective-permute-start | bytes 3080 | tf_op jit(solution)/shard_map/ppermute | solution.py:33
  10.5 14.6 %copy-start.9 = (bf16[64,1,512]{2,1,0:T(2,128)(2,1)}, bf16[64,1,512]{2,1,0:T(2,128)(2,1)S(1)}, u32[]{:S(2)}) copy-start(bf16[64,1,512]{2,1,0:T(2,128)(2,1)S(1)} %get-tuple-element.61) | copy-start | bytes 196612
  10.5 14.6 %copy-start.11 = (bf16[64,1,512]{2,1,0:T(2,128)(2,1)}, bf16[64,1,512]{2,1,0:T(2,128)(2,1)S(1)}, u32[]{:S(2)}) copy-start(bf16[64,1,512]{2,1,0:T(2,128)(2,1)S(1)} %get-tuple-element.60) | copy-start | bytes 196612
  25.4 1.6 copy-start.25
  25.8 2.6 %copy-start.3 = (bf16[768,384]{1,0:T(8,128)(2,1)S(1)}, bf16[768,384]{1,0:T(8,128)(2,1)}, u32[]{:S(2)}) copy-start(bf16[768,384]{1,0:T(8,128)(2,1)} %param.11) | copy-start | bytes 1769476
  27.0 1.6 copy-start.5
  27.0 14.0 %copy-start.2 = (bf16[768,384]{1,0:T(8,128)(2,1)S(1)}, bf16[768,384]{1,0:T(8,128)(2,1)}, u32[]{:S(2)}) copy-start(bf16[768,384]{1,0:T(8,128)(2,1)} %param.10) | copy-start | bytes 1769476
  28.4 13.6 %copy-start.7 = (bf16[64,768]{1,0:T(8,128)(2,1)}, bf16[64,768]{1,0:T(8,128)(2,1)S(1)}, u32[]{:S(2)}) copy-start(bf16[64,768]{1,0:T(8,128)(2,1)S(1)} %convolution_convert_fusion.4) | copy-start | bytes 294916
  42.0 5.0 %copy-start.4 = (bf16[768,384]{1,0:T(8,128)(2,1)S(1)}, bf16[768,384]{1,0:T(8,128)(2,1)}, u32[]{:S(2)}) copy-start(bf16[768,384]{1,0:T(8,128)(2,1)} %param.12) | copy-start | bytes 1769476
  42.0 5.0 %copy-start.8 = (bf16[64,768]{1,0:T(8,128)(2,1)S(1)}, bf16[64,768]{1,0:T(8,128)(2,1)}, u32[]{:S(2)}) copy-start(bf16[64,768]{1,0:T(8,128)(2,1)} %copy-done.7) | copy-start | bytes 294916
  44.4 17.5 %copy-start.19 = (f32[64,6]{0,1:T(8,128)}, f32[64,6]{0,1:T(8,128)S(1)}, u32[]{:S(2)}) copy-start(f32[64,6]{0,1:T(8,128)S(1)} %get-tuple-element.62) | copy-start | bytes 4612
  44.4 31.1 %collective-permute-start.1 = (f32[64,6]{0,1:T(8,128)S(1)}, f32[64,6]{0,1:T(8,128)}, u32[]{:S(2)}, u32[]{:S(2)}) collective-permute-start(f32[64,6]{0,1:T(8,128)S(1)} %get-tuple-element.62), channel_id=1, source_target_pairs={{0,1},{1,2},{2,3},{3,4},{4,5},{5,6},{6,7},{7,0},{8,9},{9,10},{10,1... | collective-permute-start | bytes 4616 | tf_op jit(solution)/shard_map/ppermute | solution.py:20
  44.8 32.4 %collective-permute-start.2 = (f32[64,6]{0,1:T(8,128)S(1)}, f32[64,6]{0,1:T(8,128)}, u32[]{:S(2)}, u32[]{:S(2)}) collective-permute-start(f32[64,6]{0,1:T(8,128)S(1)} %get-tuple-element.62), channel_id=1, source_target_pairs={{0,7},{1,0},{2,1},{3,2},{4,3},{5,4},{6,5},{7,6},{8,15},{9,8},{10,9... | collective-permute-start | bytes 4616 | tf_op jit(solution)/shard_map/ppermute | solution.py:23
  75.5 4.1 %collective-permute-start.3 = (f32[64,6]{0,1:T(8,128)}, f32[64,6]{0,1:T(8,128)S(1)}, u32[]{:S(2)}, u32[]{:S(2)}) collective-permute-start(f32[64,6]{0,1:T(8,128)} %collective-permute-done.1), channel_id=1, source_target_pairs={{0,1},{1,2},{2,3},{3,4},{4,5},{5,6},{6,7},{7,0},{8,9},{9,10},{10,1... | collective-permute-start | bytes 4616 | tf_op jit(solution)/shard_map/ppermute | solution.py:20
  77.2 4.6 %collective-permute-start.4 = (f32[64,6]{0,1:T(8,128)}, f32[64,6]{0,1:T(8,128)}, u32[]{:S(2)}, u32[]{:S(2)}) collective-permute-start(f32[64,6]{0,1:T(8,128)} %collective-permute-done.2), channel_id=1, source_target_pairs={{0,7},{1,0},{2,1},{3,2},{4,3},{5,4},{6,5},{7,6},{8,15},{9,8},{10,9... | collective-permute-start | bytes 4616 | tf_op jit(solution)/shard_map/ppermute | solution.py:23
  79.7 18.0 %copy-start.24 = (f32[64,6]{0,1:T(8,128)}, f32[64,6]{0,1:T(8,128)S(1)}, u32[]{:S(2)}) copy-start(f32[64,6]{0,1:T(8,128)S(1)} %collective-permute-done.3) | copy-start | bytes 4612
  79.7 4.8 %collective-permute-start.5 = (f32[64,6]{0,1:T(8,128)S(1)}, f32[64,6]{0,1:T(8,128)}, u32[]{:S(2)}, u32[]{:S(2)}) collective-permute-start(f32[64,6]{0,1:T(8,128)S(1)} %collective-permute-done.3), channel_id=1, source_target_pairs={{0,1},{1,2},{2,3},{3,4},{4,5},{5,6},{6,7},{7,0},{8,9},{9,10},{10,1... | collective-permute-start | bytes 4616 | tf_op jit(solution)/shard_map/ppermute | solution.py:20
  81.8 22.2 %collective-permute-start.6 = (f32[64,6]{0,1:T(8,128)}, f32[64,6]{0,1:T(8,128)}, u32[]{:S(2)}, u32[]{:S(2)}) collective-permute-start(f32[64,6]{0,1:T(8,128)} %collective-permute-done.4), channel_id=1, source_target_pairs={{0,7},{1,0},{2,1},{3,2},{4,3},{5,4},{6,5},{7,6},{8,15},{9,8},{10,9... | collective-permute-start | bytes 4616 | tf_op jit(solution)/shard_map/ppermute | solution.py:23
  84.4 20.5 %collective-permute-start.7 = (f32[64,6]{0,1:T(8,128)}, f32[64,6]{0,1:T(8,128)}, u32[]{:S(2)}, u32[]{:S(2)}) collective-permute-start(f32[64,6]{0,1:T(8,128)} %collective-permute-done.5), channel_id=1, source_target_pairs={{0,1},{1,2},{2,3},{3,4},{4,5},{5,6},{6,7},{7,0},{8,9},{9,10},{10,1... | collective-permute-start | bytes 4616 | tf_op jit(solution)/shard_map/ppermute | solution.py:20
  110.5 3.3 %copy-start.6 = (f32[64,512]{1,0:T(8,128)S(1)}, f32[64,512]{1,0:T(8,128)}, u32[]{:S(2)}) copy-start(f32[64,512]{1,0:T(8,128)} %copy-done.5) | copy-start | bytes 393220
  110.5 3.3 %copy-start.18 = (f32[64,512]{1,0:T(8,128)S(1)}, f32[64,512]{1,0:T(8,128)}, u32[]{:S(2)}) copy-start(f32[64,512]{1,0:T(8,128)} %get-tuple-element.65) | copy-start | bytes 393220
  110.5 3.4 %copy-start.21 = (f32[64]{0:T(128)S(1)}, f32[64]{0:T(128)}, u32[]{:S(2)}) copy-start(f32[64]{0:T(128)} %copy-done.20) | copy-start | bytes 772
  110.5 3.4 %copy-start.23 = (f32[64]{0:T(128)S(1)}, f32[64]{0:T(128)}, u32[]{:S(2)}) copy-start(f32[64]{0:T(128)} %copy-done.22) | copy-start | bytes 772
  110.5 3.5 %copy-start.12 = (bf16[64,1,512]{2,1,0:T(2,128)(2,1)S(1)}, bf16[64,1,512]{2,1,0:T(2,128)(2,1)}, u32[]{:S(2)}) copy-start(bf16[64,1,512]{2,1,0:T(2,128)(2,1)} %copy-done.11) | copy-start | bytes 196612
  112.0 2.3 %copy-start.10 = (bf16[64,1,512]{2,1,0:T(2,128)(2,1)S(1)}, bf16[64,1,512]{2,1,0:T(2,128)(2,1)}, u32[]{:S(2)}) copy-start(bf16[64,1,512]{2,1,0:T(2,128)(2,1)} %copy-done.9) | copy-start | bytes 196612
  112.0 2.7 %copy-start.17 = (bf16[63,1,512]{2,0,1:T(8,128)(2,1)S(1)}, bf16[63,1,512]{2,0,1:T(8,128)(2,1)}, u32[]{:S(2)}) copy-start(bf16[63,1,512]{2,0,1:T(8,128)(2,1)} %copy-done.16) | copy-start | bytes 193540
  112.0 2.7 %copy-start.26 = (bf16[1,512]{1,0:T(2,128)(2,1)S(1)}, bf16[1,512]{1,0:T(2,128)(2,1)}, u32[]{:S(2)}) copy-start(bf16[1,512]{1,0:T(2,128)(2,1)} %copy-done.25) | copy-start | bytes 3076
  116.3 60.6 %reduce-scatter.7.cloned.1.call-start = ((), (), s32[]{:S(2)}) async-start(), calls=%async_computation.3 | async-start | bytes 327680
  116.4 40.4 %collective-permute-start.8 = (bf16[1,512]{1,0:T(2,128)(2,1)S(1)}, bf16[1,512]{1,0:T(2,128)(2,1)S(1)}, u32[]{:S(2)}, u32[]{:S(2)}) collective-permute-start(bf16[1,512]{1,0:T(2,128)(2,1)S(1)} %slice.53), channel_id=1, source_target_pairs={{0,1},{1,2},{2,3},{3,4},{4,5},{5,6},{6,7},{8,9},{9,10},{10,11},{11... | collective-permute-start | bytes 3080 | tf_op jit(solution)/shard_map/ppermute | solution.py:33
  (6 other events, 3.7 us)
Sparse Core Ops, SparseCore 0:
  116.4 38.5 reduce-scatter.4
  157.2 19.6 reduce-scatter.6
